TPU v7x, 1024 devices: a whole 4x4x32 slice. The times are simulated.
1024 devices in a mesh: group: 64 (over z, core), node: 16 (over y, x).
Axes of the slice: x: 4, y: 4, z: 32, core: 2. Of those that a mesh axis runs over, the one named last changes fastest.
Arguments:
- grads: bfloat16 [393216, 1280], P(('group', 'node')), may hold values from -6 to 6
- merge_slot: int32 [393216], P(('group', 'node')), may hold values from 0 to 383, as said below
- slot_row: int32 [393216], P(('group', 'node')), may hold values from 0 to 63, as said below
- params: float32 [65536, 1280], P(('group', 'node')), may hold values from -6 to 6
- moment: float32 [65536, 1280], P(('group', 'node')), may hold values from -4 to 4
- second: float32 [65536, 1280], P(('group', 'node')), may hold values from 0.01 to 1
Outputs:
- new_params: float32 [65536, 1280], P(('group', 'node'))
- new_moment: float32 [65536, 1280], P(('group', 'node'))
- new_second: float32 [65536, 1280], P(('group', 'node'))
Inputs may be any that keep to these rules, and one draw needn't show every extreme that they name: `merge_slot`: tokens of one merging device that share a slot share a table row; slot s of merging device (g, k) goes to owner (s // 6, k); slot 0 and slot 383 are used on every merging device. `slot_row`: within each aligned block of 6 slots of one merging device the rows are distinct.
All inputs are finite; a program needn't handle non-finite values.
Results may differ from a plain program's by a relative error of at most 0.0003.
Values may be sent and summed in bfloat16 or wider, within the bound.
A program may use at most 128 MiB of HBM per device.

v0:
```python
import jax
import jax.numpy as jnp
from jax import lax
from jax.sharding import PartitionSpec as P


def on_device(grads, merge_slot, slot_row, params, moment, second):
    tokens_here = grads.shape[0]
    rows_here = params.shape[0]
    arrived_tokens, arrived_slots = (
        lax.all_to_all(grads, "node", split_axis=0, concat_axis=0, tiled=True),
        lax.all_to_all(merge_slot, "node", split_axis=0, concat_axis=0, tiled=True),
    )
    slots_iota = lax.broadcasted_iota(jnp.int32, (tokens_here, tokens_here), 0)
    onehot = (arrived_slots[None, :] == slots_iota).astype(jnp.bfloat16)
    merged = jnp.dot(onehot, arrived_tokens, preferred_element_type=jnp.float32)
    arrived_rows, arrived_index = (
        lax.all_to_all(merged, "group", split_axis=0, concat_axis=0, tiled=True),
        lax.all_to_all(slot_row, "group", split_axis=0, concat_axis=0, tiled=True),
    )
    rows_iota = lax.broadcasted_iota(jnp.int32, (rows_here, tokens_here), 0)
    placing = (arrived_index[None, :] == rows_iota).astype(jnp.float32)
    grad = jnp.dot(
        placing, arrived_rows, precision=lax.Precision.HIGHEST, preferred_element_type=jnp.float32
    )
    new_moment = 0.9 * moment + 0.1 * grad
    new_second = 0.999 * second + 0.001 * grad * grad
    first_fix = 1.0 - 0.9**10
    second_fix = 1.0 - 0.999**10
    new_params = params - 0.1 * (new_moment / first_fix) / (
        jnp.sqrt(new_second / second_fix) + 1e-08
    )
    return (new_params, new_moment, new_second)


def solution(mesh):
    placed = (
        P(("group", "node"), None),
        P(("group", "node")),
        P(("group", "node")),
        P(("group", "node"), None),
        P(("group", "node"), None),
        P(("group", "node"), None),
    )
    return jax.shard_map(
        on_device,
        mesh=mesh,
        in_specs=placed,
        out_specs=(
            P(("group", "node"), None),
            P(("group", "node"), None),
            P(("group", "node"), None),
        ),
        check_vma=False,
    )
```

profile of v0, /device:TPU:2, one launch (start us, length us, event | category | flops | bytes accessed | tf_op | source)
XLA Modules:
  0.0 342.1 jit_solution(7068978409000392692)
XLA Ops:
  0.6 0.0 copy-start.2
  0.6 0.8 all_to_all.28
  1.4 22.0 %all_to_all.39 = s32[16,24,1]{1,2,0:T(1,128)S(1)} all-to-all(s32[16,24,1]{1,2,0:T(1,128)S(1)} %bitcast.12), channel_id=1, replica_groups=mesh['group'=64,'node'=16] {'node'}, dimensions={0} | all-to-all | bytes 3072 | tf_op jit(solution)/shard_map/all_to_all | solution.py:12
  23.4 4.7 %all-to-all-start.2 = ((bf16[16,24,1280]{2,1,0:T(8,128)(2,1)}), bf16[16,24,1280]{2,1,0:T(8,128)(2,1)S(1)}, u32[]{:S(2)}, u32[]{:S(2)}) async-start(bf16[16,24,1280]{2,1,0:T(8,128)(2,1)} %bitcast.11), calls=%async_computation.2 | async-start | bytes 1966080 | tf_op jit(solution)/shard_map/all_to_all | solution.py:11
  28.1 0.0 copy-done.2
  28.1 0.8 all_to_all.26
  28.9 0.5 broadcast.33
  29.4 0.7 reduce.6
  30.1 0.1 eq.28
  30.2 9.6 %all-to-all-done.2 = bf16[16,24,1280]{2,1,0:T(8,128)(2,1)S(1)} async-done(((bf16[16,24,1280]{2,1,0:T(8,128)(2,1)}), bf16[16,24,1280]{2,1,0:T(8,128)(2,1)S(1)}, u32[]{:S(2)}, u32[]{:S(2)}) %all-to-all-start.2) | async-done | bytes 983072 | tf_op jit(solution)/shard_map/all_to_all | solution.py:11
  39.8 23.7 %all-to-all-start = ((s32[64,6,1]{1,2,0:T(1,128)}), s32[64,6,1]{1,2,0:T(1,128)S(1)}, u32[]{:S(2)}, u32[]{:S(2)}) async-start(s32[64,6,1]{1,2,0:T(1,128)} %bitcast), calls=%async_computation | async-start | bytes 65536 | tf_op jit(solution)/shard_map/all_to_all | solution.py:19
  63.5 0.7 fusion
  64.2 2.7 copy.12
  66.9 20.1 %all-to-all-done = s32[64,6,1]{1,2,0:T(1,128)S(1)} async-done(((s32[64,6,1]{1,2,0:T(1,128)}), s32[64,6,1]{1,2,0:T(1,128)S(1)}, u32[]{:S(2)}, u32[]{:S(2)}) %all-to-all-start) | async-done | bytes 1568 | tf_op jit(solution)/shard_map/all_to_all | solution.py:19
  87.0 4.7 %all-to-all-start.3 = ((f32[64,6,1280]{2,1,0:T(8,128)}), f32[64,6,1280]{2,1,0:T(8,128)S(1)}, u32[]{:S(2)}, u32[]{:S(2)}) async-start(f32[64,6,1280]{2,1,0:T(8,128)} %copy.12), calls=%async_computation.3 | async-start | bytes 5242880 | tf_op jit(solution)/shard_map/all_to_all | solution.py:18
  91.7 0.7 reduce.7
  92.4 0.1 eq.25
  92.6 0.0 copy-start
  92.6 0.0 copy-start.1
  92.6 244.6 %all-to-all-done.3 = f32[64,6,1280]{2,1,0:T(8,128)S(1)} async-done(((f32[64,6,1280]{2,1,0:T(8,128)}), f32[64,6,1280]{2,1,0:T(8,128)S(1)}, u32[]{:S(2)}, u32[]{:S(2)}) %all-to-all-start.3) | async-done | bytes 1966112 | tf_op jit(solution)/shard_map/all_to_all | solution.py:18
  337.2 1.4 all_to_all.34
  338.7 0.0 copy-done
  338.7 0.0 copy-done.1
  338.7 3.4 divide_subtract_fusion
  (1 shorter events, 0.0 us)
Async XLA Ops:
  0.6 27.5 %copy-start.2 = (s32[384]{0:T(512)S(1)}, s32[384]{0:T(512)}, u32[]{:S(2)}) copy-start(s32[384]{0:T(512)} %param.8) | copy-start | bytes 4612
  23.4 16.3 %all-to-all-start.2 = ((bf16[16,24,1280]{2,1,0:T(8,128)(2,1)}), bf16[16,24,1280]{2,1,0:T(8,128)(2,1)S(1)}, u32[]{:S(2)}, u32[]{:S(2)}) async-start(bf16[16,24,1280]{2,1,0:T(8,128)(2,1)} %bitcast.11), calls=%async_computation.2 | async-start | bytes 1966080 | tf_op jit(solution)/shard_map/all_to_all | solution.py:11
  39.8 47.2 %all-to-all-start = ((s32[64,6,1]{1,2,0:T(1,128)}), s32[64,6,1]{1,2,0:T(1,128)S(1)}, u32[]{:S(2)}, u32[]{:S(2)}) async-start(s32[64,6,1]{1,2,0:T(1,128)} %bitcast), calls=%async_computation | async-start | bytes 65536 | tf_op jit(solution)/shard_map/all_to_all | solution.py:19
  87.0 250.3 %all-to-all-start.3 = ((f32[64,6,1280]{2,1,0:T(8,128)}), f32[64,6,1280]{2,1,0:T(8,128)S(1)}, u32[]{:S(2)}, u32[]{:S(2)}) async-start(f32[64,6,1280]{2,1,0:T(8,128)} %copy.12), calls=%async_computation.3 | async-start | bytes 5242880 | tf_op jit(solution)/shard_map/all_to_all | solution.py:18
  92.6 246.1 %copy-start = (f32[64,1280]{1,0:T(8,128)S(1)}, f32[64,1280]{1,0:T(8,128)}, u32[]{:S(2)}) copy-start(f32[64,1280]{1,0:T(8,128)} %param.9) | copy-start | bytes 983044
  92.6 246.1 %copy-start.1 = (f32[64,1280]{1,0:T(8,128)S(1)}, f32[64,1280]{1,0:T(8,128)}, u32[]{:S(2)}) copy-start(f32[64,1280]{1,0:T(8,128)} %param.10) | copy-start | bytes 983044
where the time goes:
time: 343 us; the launch traced here: 342 us
  waiting for transfers between devices  274 us (80%)
  starting transfers between devices  33.1 us (10%)
  blocking collectives  22 us (6%)
  local copies, waits for them, and re-layouts  6.39 us (2%)
  matrix products  4.12 us (1%)
    all_to_all x1, waiting for transfers between devices, on_device(): lax.all_to_all(merged, 'group', split_axis=0, concat_axis=0, tiled=True)  245 us
    all_to_all x1, starting transfers between devices, on_device(): lax.all_to_all(slot_row, 'group', split_axis=0, concat_axis=0, tiled=True)  23.7 us
    all_to_all x1, blocking collectives, on_device(): lax.all_to_all(merge_slot, 'node', split_axis=0, concat_axis=0, tiled=True)  22 us
    all_to_all x1, waiting for transfers between devices, on_device(): lax.all_to_all(slot_row, 'group', split_axis=0, concat_axis=0, tiled=True)  20.1 us
    all_to_all x1, waiting for transfers between devices, on_device(): lax.all_to_all(grads, 'node', split_axis=0, concat_axis=0, tiled=True)  9.59 us
  transfers between devices with their start and end apart: 3, of which 3 were waited for; matrix products, arithmetic and copies ran while one was open for 2% of the time, Pallas kernels for 0%

commit v1 on v0

v1 whole, which is shorter than its diff:
```python
import functools

import jax
import jax.numpy as jnp
from jax import lax
from jax.experimental import pallas as pl
from jax.experimental.pallas import tpu as pltpu
from jax.sharding import PartitionSpec as P

MESH = pl.DeviceIdType.MESH
LANES = 128
PAIR = 2 * LANES
SUBS = (3, 2)
FINE = 64.0
TOP = 32600.0
LONGER, SHORTER = 0, 1


def block_rows(chunks, rows):
    return -(-(chunks * rows + chunks) // 8) * 8


def quotient(x, by, limit):
    magic = -(-65536 // by)
    assert all((v * magic) >> 16 == v // by for v in range(limit))
    return (x * magic) >> 16


def low_half(p):
    return (p << 16) >> 16


def pack(hi, lo):
    return (hi << 16) | (lo & 0xFFFF)


def nearest(x):
    return jnp.floor(x + 0.5).astype(jnp.int32)


def level_of(x):
    most = jnp.max(jnp.abs(x), axis=0, keepdims=True)
    return jnp.ceil(jnp.log2(jnp.maximum(most, 1e-30)) * FINE)


def quantise(x):
    level = level_of(x)
    q = nearest(x * (jnp.exp2(level * (-1.0 / FINE)) * TOP))
    return q, level.astype(jnp.int32)


def step_size(level):
    return jnp.exp2(level.astype(jnp.float32) * (1.0 / FINE)) * (1.0 / TOP)


def kernel(
    cfg,
    grads,
    slots,
    slot_row,
    out,
    tok3,
    slot_in,
    tok,
    code,
    contrib,
    slot_mat,
    *rest,
):
    n_group, n_node, rows, toks, width = cfg
    n_sub = len(SUBS)
    sends, rest = rest[:n_sub], rest[n_sub:]
    recvs, rest = rest[:n_sub], rest[n_sub:]
    (
        slot_send_sem,
        slot_recv_sem,
        tok_send_sem,
        tok_recv_sem,
        local_sem,
        pair_send_sem,
        pair_recv_sem,
        ring_send_sem,
        ring_recv_sem,
    ) = rest
    nz = n_group // 2
    hops = (nz // 2, nz // 2 - 1)
    blk = toks // n_node
    cap = toks // n_group
    starts = [PAIR * sum(SUBS[:i]) for i in range(n_sub)]
    cols = [slice(starts[i], starts[i] + PAIR * SUBS[i]) for i in range(n_sub)]

    group = lax.axis_index("group")
    node = lax.axis_index("node")
    z, c = lax.div(group, 2), lax.rem(group, 2)
    sign = 1 - 2 * c
    toward = (sign, -sign)

    def at_z(pos):
        return lax.rem(pos + 2 * nz, nz)

    partner = (z * 2 + 1 - c, node)
    ahead = [(at_z(z + toward[d]) * 2 + c, node) for d in (LONGER, SHORTER)]

    barrier = pltpu.get_barrier_semaphore()

    @pl.loop(1, n_node)
    def _(j):
        pl.semaphore_signal(
            barrier,
            inc=1,
            device_id=(group, lax.rem(node + j, n_node)),
            device_id_type=MESH,
        )

    for other in (partner, *ahead):
        pl.semaphore_signal(barrier, inc=1, device_id=other, device_id_type=MESH)
    pl.semaphore_wait(barrier, n_node + 2)

    def slot_copy(j):
        peer = lax.rem(node + j, n_node)
        return pltpu.make_async_remote_copy(
            src_ref=slots,
            dst_ref=slot_in.at[node],
            send_sem=slot_send_sem.at[j],
            recv_sem=slot_recv_sem.at[node],
            device_id=(group, peer),
            device_id_type=MESH,
        )

    def slot_arrival(j):
        peer = lax.rem(node + j, n_node)
        return pltpu.make_async_remote_copy(
            src_ref=slots,
            dst_ref=slot_in.at[peer],
            send_sem=slot_send_sem.at[j],
            recv_sem=slot_recv_sem.at[peer],
            device_id=(group, peer),
            device_id_type=MESH,
        )

    def tok_copy(i, j):
        peer = lax.rem(node + j, n_node)
        return pltpu.make_async_remote_copy(
            src_ref=grads.at[peer, :, cols[i]],
            dst_ref=tok3.at[node, :, cols[i]],
            send_sem=tok_send_sem.at[i, j],
            recv_sem=tok_recv_sem.at[i, node],
            device_id=(group, peer),
            device_id_type=MESH,
        )

    def tok_arrival(i, j):
        peer = lax.rem(node + j, n_node)
        return pltpu.make_async_remote_copy(
            src_ref=grads.at[peer, :, cols[i]],
            dst_ref=tok3.at[peer, :, cols[i]],
            send_sem=tok_send_sem.at[i, j],
            recv_sem=tok_recv_sem.at[i, peer],
            device_id=(group, peer),
            device_id_type=MESH,
        )

    own_tok = pltpu.make_async_copy(grads.at[node], tok3.at[node], local_sem.at[0])
    own_slot = pltpu.make_async_copy(slots, slot_in.at[node], local_sem.at[1])

    @pl.loop(1, n_node)
    def _(j):
        slot_copy(j).start()

    own_slot.start()
    own_tok.start()
    for i in range(n_sub):

        @pl.loop(1, n_node)
        def _(j, i=i):
            tok_copy(i, j).start()

    own_slot.wait()

    @pl.loop(1, n_node)
    def _(j):
        slot_arrival(j).wait_recv()

    for n in range(n_node):
        slot_mat[n : n + 1, :] = slot_in[n]
    slot = slot_mat[...]
    owner = quotient(slot, cap, toks)
    place = slot - owner * cap
    lane = lax.broadcasted_iota(jnp.int32, (toks, toks), 1)
    sub = lax.broadcasted_iota(jnp.int32, (toks, toks), 0)
    mine = (sub - node * blk == lane - quotient(lane, blk, toks) * blk).astype(
        jnp.bfloat16
    )
    lane = lax.broadcasted_iota(jnp.int32, (n_node, toks), 1)
    source = lax.broadcasted_iota(jnp.int32, (n_node, toks), 0)
    here = (quotient(lane, blk, toks) == source).astype(jnp.float32)

    def pick(values):
        moved = jnp.dot(
            values.astype(jnp.float32).astype(jnp.bfloat16),
            mine,
            preferred_element_type=jnp.float32,
        )
        return jnp.sum(moved * here, axis=0, keepdims=True)

    owner = pick(owner)
    index = owner * float(cap) + pick(place)
    onehot = (index == sub.astype(jnp.float32)).astype(jnp.bfloat16)
    table = jnp.broadcast_to(slot_row[...], (8, toks)).astype(jnp.float32)
    row = jnp.dot(
        table.astype(jnp.bfloat16), onehot, preferred_element_type=jnp.float32
    )
    code[0] = owner * float(rows) + row[0:1, :]

    pair_code = pltpu.make_async_remote_copy(
        src_ref=code.at[0],
        dst_ref=code.at[1],
        send_sem=pair_send_sem.at[n_sub],
        recv_sem=pair_recv_sem.at[n_sub],
        device_id=partner,
        device_id_type=MESH,
    )
    pair_code.start()

    def pair_copy(i):
        return pltpu.make_async_remote_copy(
            src_ref=tok.at[0:toks, cols[i]],
            dst_ref=tok.at[toks : 2 * toks, cols[i]],
            send_sem=pair_send_sem.at[i],
            recv_sem=pair_recv_sem.at[i],
            device_id=partner,
            device_id_type=MESH,
        )

    def onehot_of(owner_z):
        base = ((owner_z * 2 + c) * rows).astype(jnp.float32)
        ids = lax.broadcasted_iota(jnp.int32, (rows, toks), 0).astype(jnp.float32)
        ids = ids + base
        return jnp.concatenate(
            [(code[h] == ids).astype(jnp.bfloat16) for h in (0, 1)], axis=1
        )

    def add_up(dst, owner_z, i):
        onehot = onehot_of(owner_z)
        for k in range(SUBS[i]):
            at = starts[i] + k * PAIR
            dst[:, at : at + PAIR] = jnp.dot(
                onehot, tok[:, at : at + PAIR], preferred_element_type=jnp.float32
            )

    def arrived(ref, i, k):
        levels = ref[rows * SUBS[i] + k : rows * SUBS[i] + k + 1, :]
        packed = ref[rows * k : rows * (k + 1), :]
        hi = (packed >> 16).astype(jnp.float32) * step_size(levels >> 16)
        lo = low_half(packed).astype(jnp.float32) * step_size(low_half(levels))
        return hi, lo

    def ring_copy(i, d, s):
        return pltpu.make_async_remote_copy(
            src_ref=sends[i].at[d, lax.rem(s, 2)],
            dst_ref=recvs[i].at[d, s],
            send_sem=ring_send_sem.at[i, d, lax.rem(s, 2)],
            recv_sem=ring_recv_sem.at[i, d, s],
            device_id=ahead[d],
            device_id_type=MESH,
        )

    def ring_step(i, d, s, first):
        owner_z = at_z(z + toward[d] * (hops[d] - s))
        add_up(contrib, owner_z, i)
        if not first:
            ring_copy(i, d, s - 1).wait_recv()

            @pl.when(s >= 2)
            def _():
                ring_copy(i, d, s - 2).wait_send()

        send = sends[i].at[d, lax.rem(s, 2)]
        for k in range(SUBS[i]):
            at = starts[i] + k * PAIR
            hi = contrib[:, at : at + LANES]
            lo = contrib[:, at + LANES : at + PAIR]
            if not first:
                more_hi, more_lo = arrived(recvs[i].at[d, s - 1], i, k)
                hi, lo = hi + more_hi, lo + more_lo
            q_hi, level_hi = quantise(hi)
            q_lo, level_lo = quantise(lo)
            send[rows * k : rows * (k + 1), :] = pack(q_hi, q_lo)
            send[rows * SUBS[i] + k : rows * SUBS[i] + k + 1, :] = pack(
                level_hi, level_lo
            )
        ring_copy(i, d, s).start()

    for i in range(n_sub):
        if i == 0:
            own_tok.wait()

        @pl.loop(1, n_node)
        def _(j, i=i):
            tok_arrival(i, j).wait_recv()

        tok[0:toks, cols[i]] = jnp.concatenate(
            [tok3[n, :, cols[i]].astype(jnp.float32) for n in range(n_node)], axis=0
        ).astype(jnp.bfloat16)
        pair_copy(i).start()
        if i == 0:
            pair_code.wait_recv()
        pair_copy(i).wait_recv()
        for d in (LONGER, SHORTER):
            ring_step(i, d, 0, True)

    @pl.loop(1, hops[SHORTER])
    def _(s):
        for i in range(n_sub):
            for d in (LONGER, SHORTER):
                ring_step(i, d, s, False)

    for i in range(n_sub):
        ring_step(i, LONGER, hops[LONGER] - 1, False)
    for i in range(n_sub):
        add_up(contrib, z, i)
    for i in range(n_sub):
        for d in (LONGER, SHORTER):
            ring_copy(i, d, hops[d] - 1).wait_recv()
        for k in range(SUBS[i]):
            at = starts[i] + k * PAIR
            hi = contrib[:, at : at + LANES]
            lo = contrib[:, at + LANES : at + PAIR]
            for d in (LONGER, SHORTER):
                more_hi, more_lo = arrived(recvs[i].at[d, hops[d] - 1], i, k)
                hi, lo = hi + more_hi, lo + more_lo
            out[:, at : at + LANES] = hi
            out[:, at + LANES : at + PAIR] = lo

    @pl.loop(1, n_node)
    def _(j):
        slot_copy(j).wait_send()
        for i in range(n_sub):
            tok_copy(i, j).wait_send()

    pair_code.wait_send()
    for i in range(n_sub):
        pair_copy(i).wait_send()
        for d in (LONGER, SHORTER):
            for s in range(max(hops[d] - 2, 0), hops[d]):
                ring_copy(i, d, s).wait_send()


def summed(grads, merge_slot, slot_row, n_group, n_node, rows):
    toks, width = grads.shape
    blk = toks // n_node
    assert width == PAIR * sum(SUBS)
    nz = n_group // 2
    hops = nz // 2
    n_sub = len(SUBS)
    cfg = (n_group, n_node, rows, toks, width)
    i32, f32, bf16 = jnp.int32, jnp.float32, jnp.bfloat16
    vmem, dma = pltpu.VMEM, pltpu.SemaphoreType.DMA
    return pl.pallas_call(
        functools.partial(kernel, cfg),
        out_shape=jax.ShapeDtypeStruct((rows, width), f32),
        in_specs=[
            pl.BlockSpec(memory_space=pl.ANY),
            pl.BlockSpec(memory_space=vmem),
            pl.BlockSpec(memory_space=vmem),
        ],
        out_specs=pl.BlockSpec(memory_space=vmem),
        scratch_shapes=[
            vmem((n_node, blk, width), bf16),
            vmem((n_node, 1, toks), i32),
            vmem((2 * toks, width), bf16),
            vmem((2, 1, toks), f32),
            vmem((rows, width), f32),
            vmem((n_node, toks), i32),
            *[vmem((2, 2, block_rows(m, rows), LANES), i32) for m in SUBS],
            *[vmem((2, hops, block_rows(m, rows), LANES), i32) for m in SUBS],
            dma((n_node,)),
            dma((n_node,)),
            dma((n_sub, n_node)),
            dma((n_sub, n_node)),
            dma((2,)),
            dma((n_sub + 1,)),
            dma((n_sub + 1,)),
            dma((n_sub, 2, 2)),
            dma((n_sub, 2, hops)),
        ],
        compiler_params=pltpu.CompilerParams(
            collective_id=0, has_side_effects=True, vmem_limit_bytes=40 * 1024 * 1024
        ),
        name="ring_sums",
    )(
        grads.reshape(n_node, blk, width),
        merge_slot.reshape(1, toks),
        slot_row.reshape(1, toks),
    )


def on_device(n_group, n_node, grads, merge_slot, slot_row, params, moment, second):
    grad = summed(grads, merge_slot, slot_row, n_group, n_node, params.shape[0])
    new_moment = 0.9 * moment + 0.1 * grad
    new_second = 0.999 * second + 0.001 * grad * grad
    first_fix = 1.0 - 0.9**10
    second_fix = 1.0 - 0.999**10
    new_params = params - 0.1 * (new_moment / first_fix) / (
        jnp.sqrt(new_second / second_fix) + 1e-08
    )
    return (new_params, new_moment, new_second)


def solution(mesh):
    whole, flat = P(("group", "node"), None), P(("group", "node"))
    return jax.shard_map(
        functools.partial(on_device, mesh.shape["group"], mesh.shape["node"]),
        mesh=mesh,
        in_specs=(whole, flat, flat, whole, whole, whole),
        out_specs=(whole, whole, whole),
        check_vma=False,
    )
```

time: 343 us -> 113 us (0.33)
  the two profiles are of different devices: /device:TPU:2 before, /device:TPU:32 now
where the time goes in v1:
time: 113 us
  Pallas kernels  109 us (96%)
  local copies, waits for them, and re-layouts  1.91 us (2%)
    pallas_call x1, Pallas kernels, summed(): pl.pallas_call(functools.partial(kernel, cfg), out_shape=jax.ShapeDtypeSt...  109 us

profile of v1, /device:TPU:32, one launch (start us, length us, event | category | flops | bytes accessed | tf_op | source)
XLA Modules:
  0.0 112.6 jit_solution(13458564424004995055)
XLA Ops:
  0.6 0.0 copy-start.4
  0.6 0.7 reshape.16.slots
  1.3 0.0 copy-done.4
  1.3 0.0 copy-start
  1.3 1.2 %copy-done = bf16[384,1280]{1,0:T(8,128)(2,1)S(1)} copy-done((bf16[384,1280]{1,0:T(8,128)(2,1)S(1)}, bf16[384,1280]{1,0:T(8,128)(2,1)}, u32[]{:S(2)}) %copy-start) | copy-done | bytes 983064
  2.5 0.0 copy-start.1
  2.5 0.0 copy-start.2
  2.5 0.0 copy-start.3
  2.5 108.9 %ring_sums.1 = f32[64,1280]{1,0:T(8,128)S(1)} custom-call(bf16[16,24,1280]{2,1,0:T(8,128)(2,1)S(1)} %bitcast.1, s32[1,384]{1,0:T(1,128)S(1)} %reshape.16.slots, s32[1,384]{1,0:T(1,128)S(1)} %reshape.17.slot_row), custom_call_target="tpu_custom_call" | custom-call | tf_op jit(solution)/shard_map/ring_sums/pallas_call | solution.py:359
  111.5 0.0 copy-done.1
  111.5 0.0 copy-done.2
  111.5 0.0 copy-done.3
  111.5 1.1 divide_subtract_fusion
  (1 shorter events, 0.0 us)
Async XLA Ops:
  0.6 0.7 copy-start.4
  1.3 1.2 %copy-start = (bf16[384,1280]{1,0:T(8,128)(2,1)S(1)}, bf16[384,1280]{1,0:T(8,128)(2,1)}, u32[]{:S(2)}) copy-start(bf16[384,1280]{1,0:T(8,128)(2,1)} %param.6) | copy-start | bytes 2949124
  2.5 109.0 %copy-start.1 = (f32[64,1280]{1,0:T(8,128)S(1)}, f32[64,1280]{1,0:T(8,128)}, u32[]{:S(2)}) copy-start(f32[64,1280]{1,0:T(8,128)} %param.9) | copy-start | bytes 983044
  2.5 109.0 %copy-start.2 = (f32[64,1280]{1,0:T(8,128)S(1)}, f32[64,1280]{1,0:T(8,128)}, u32[]{:S(2)}) copy-start(f32[64,1280]{1,0:T(8,128)} %param.10) | copy-start | bytes 983044
  2.5 109.0 %copy-start.3 = (f32[64,1280]{1,0:T(8,128)S(1)}, f32[64,1280]{1,0:T(8,128)}, u32[]{:S(2)}) copy-start(f32[64,1280]{1,0:T(8,128)} %param.11) | copy-start | bytes 983044

commit v2 on v1

v2 whole, which is shorter than its diff:
```python
import functools

import jax
import jax.numpy as jnp
from jax import lax
from jax.experimental import pallas as pl
from jax.experimental.pallas import tpu as pltpu
from jax.sharding import PartitionSpec as P

MESH = pl.DeviceIdType.MESH
LANES = 128
PIECE = 2 * LANES
FINE = 64.0
TOP = 32600.0
LONGER, SHORTER = 0, 1


def quotient(x, by, limit):
    magic = -(-65536 // by)
    assert all((v * magic) >> 16 == v // by for v in range(limit))
    return (x * magic) >> 16


def low_half(p):
    return (p << 16) >> 16


def pack(hi, lo):
    return (hi << 16) | (lo & 0xFFFF)


def nearest(x):
    return jnp.floor(x + 0.5).astype(jnp.int32)


def halves(x):
    return x[..., :LANES], x[..., LANES:]


def quantise(x):
    most = jnp.max(jnp.abs(x), axis=-2, keepdims=True)
    level = jnp.ceil(jnp.log2(jnp.maximum(most, 1e-30)) * FINE)
    q = nearest(x * (jnp.exp2(level * (-1.0 / FINE)) * TOP))
    return pack(*halves(q)), pack(*halves(level.astype(jnp.int32)))


def step_size(level):
    return jnp.exp2(level.astype(jnp.float32) * (1.0 / FINE)) * (1.0 / TOP)


def unpack(packed, levels):
    hi = (packed >> 16).astype(jnp.float32) * step_size(levels >> 16)
    lo = low_half(packed).astype(jnp.float32) * step_size(low_half(levels))
    return jnp.concatenate([hi, lo], axis=-1)


def plan(n_group, toks):
    nz = n_group // 2
    hops = (nz // 2, nz // 2 - 1)
    relay = 12 if nz == 32 else max(nz // 2 - 2, 1)
    far = (hops[0] - relay, hops[1] - relay)
    both = 2 * (toks // n_group)
    return nz, relay, far, both, -(-(both + 2) // 8) * 8


def kernel(
    cfg,
    grads,
    slots,
    slot_row,
    out,
    tok3,
    slot_in,
    tok,
    code,
    slot_mat,
    onehots,
    contrib,
    far_onehot,
    far_ids,
    far_out,
    far_in,
    ring_out,
    ring_in,
    slot_send_sem,
    slot_recv_sem,
    tok_send_sem,
    tok_recv_sem,
    local_sem,
    pair_send_sem,
    pair_recv_sem,
    far_send_sem,
    far_recv_sem,
    ring_send_sem,
    ring_recv_sem,
):
    n_group, n_node, rows, toks, width = cfg
    nz, relay, far, both, far_rows = plan(n_group, toks)
    f32, bf16 = jnp.float32, jnp.bfloat16
    pieces = width // PIECE
    blk = toks // n_node
    cap = toks // n_group
    cols = [slice(PIECE * i, PIECE * (i + 1)) for i in range(pieces)]
    ways = (LONGER, SHORTER)
    far_all = far[LONGER] + far[SHORTER]

    group = lax.axis_index("group")
    node = lax.axis_index("node")
    z, c = lax.div(group, 2), lax.rem(group, 2)
    sign = 1 - 2 * c
    toward = (sign, -sign)

    def at_z(pos):
        return lax.rem(pos + 2 * nz, nz)

    def along(d, distance):
        return at_z(z + toward[d] * distance) * 2 + c

    partner = (z * 2 + 1 - c, node)

    far_in[...] = jnp.zeros_like(far_in)
    barrier = pltpu.get_barrier_semaphore()

    @pl.loop(1, n_node)
    def _(j):
        pl.semaphore_signal(
            barrier,
            inc=1,
            device_id=(group, lax.rem(node + j, n_node)),
            device_id_type=MESH,
        )

    near = max(far[LONGER], 1)
    pl.semaphore_signal(barrier, inc=1, device_id=partner, device_id_type=MESH)
    for d in ways:

        @pl.loop(1, near + 1)
        def _(j, d=d):
            pl.semaphore_signal(
                barrier, inc=1, device_id=(along(d, j), node), device_id_type=MESH
            )

    pl.semaphore_wait(barrier, n_node + 2 * near)

    def slot_copy(j, landing):
        peer = lax.rem(node + j, n_node)
        at = peer if landing else node
        return pltpu.make_async_remote_copy(
            src_ref=slots,
            dst_ref=slot_in.at[at],
            send_sem=slot_send_sem.at[j],
            recv_sem=slot_recv_sem.at[at],
            device_id=(group, peer),
            device_id_type=MESH,
        )

    def tok_copy(i, j, landing):
        peer = lax.rem(node + j, n_node)
        at = peer if landing else node
        return pltpu.make_async_remote_copy(
            src_ref=grads.at[peer, :, cols[i]],
            dst_ref=tok3.at[at, :, cols[i]],
            send_sem=tok_send_sem.at[i, j],
            recv_sem=tok_recv_sem.at[i, at],
            device_id=(group, peer),
            device_id_type=MESH,
        )

    own_tok = pltpu.make_async_copy(grads.at[node], tok3.at[node], local_sem.at[0])
    own_slot = pltpu.make_async_copy(slots, slot_in.at[node], local_sem.at[1])

    @pl.loop(1, n_node)
    def _(j):
        slot_copy(j, False).start()

    own_slot.start()
    own_tok.start()
    for i in range(pieces):

        @pl.loop(1, n_node)
        def _(j, i=i):
            tok_copy(i, j, False).start()

    own_slot.wait()

    @pl.loop(1, n_node)
    def _(j):
        slot_copy(j, True).wait_recv()

    for n in range(n_node):
        for k in range(toks // LANES):
            slot_mat[n : n + 1, k * LANES : (k + 1) * LANES] = slot_in[n, k : k + 1, :]
    slot = slot_mat[...]
    owner = quotient(slot, cap, toks)
    place = slot - owner * cap
    lane = lax.broadcasted_iota(jnp.int32, (toks, toks), 1)
    sub = lax.broadcasted_iota(jnp.int32, (toks, toks), 0)
    mine = sub - node * blk == lane - quotient(lane, blk, toks) * blk
    mine = mine.astype(f32).astype(bf16)
    lane = lax.broadcasted_iota(jnp.int32, (n_node, toks), 1)
    source = lax.broadcasted_iota(jnp.int32, (n_node, toks), 0)
    here = (quotient(lane, blk, toks) == source).astype(f32)

    def pick(values):
        moved = jnp.dot(
            values.astype(f32).astype(bf16), mine, preferred_element_type=f32
        )
        return jnp.sum(moved * here, axis=0, keepdims=True)

    owner = pick(owner)
    index = owner * float(cap) + pick(place)
    onehot = (index == sub.astype(f32)).astype(f32).astype(bf16)
    table = jnp.concatenate(
        [slot_row[k : k + 1, :] for k in range(toks // LANES)], axis=1
    ).astype(f32)
    row = jnp.dot(
        jnp.broadcast_to(table, (8, toks)).astype(bf16),
        onehot,
        preferred_element_type=f32,
    )
    code[0, 0:1, :] = owner * float(rows) + row[0:1, :]
    code[0, 1:2, :] = index
    code[0, 2:3, :] = table

    pair_code = pltpu.make_async_remote_copy(
        src_ref=code.at[0],
        dst_ref=code.at[1],
        send_sem=pair_send_sem.at[pieces],
        recv_sem=pair_recv_sem.at[pieces],
        device_id=partner,
        device_id_type=MESH,
    )
    pair_code.start()

    def pair_copy(i):
        return pltpu.make_async_remote_copy(
            src_ref=tok.at[0:toks, cols[i]],
            dst_ref=tok.at[toks : 2 * toks, cols[i]],
            send_sem=pair_send_sem.at[i],
            recv_sem=pair_recv_sem.at[i],
            device_id=partner,
            device_id_type=MESH,
        )

    def far_copy(i, k):
        d, j = (LONGER, k) if k < far[LONGER] else (SHORTER, k - far[LONGER])
        return pltpu.make_async_remote_copy(
            src_ref=far_out.at[i, k, 0 : both + 2],
            dst_ref=far_in.at[i, k, 0 : both + 2],
            send_sem=far_send_sem.at[i, k],
            recv_sem=far_recv_sem.at[i, k],
            device_id=(along(d, j + 1), node),
            device_id_type=MESH,
        )

    def ring_copy(i, d, s):
        return pltpu.make_async_remote_copy(
            src_ref=ring_out.at[i, lax.rem(s, 2), d],
            dst_ref=ring_in.at[i, s, d],
            send_sem=ring_send_sem.at[i, d, lax.rem(s, 2)],
            recv_sem=ring_recv_sem.at[i, d, s],
            device_id=(along(d, 1), node),
            device_id_type=MESH,
        )

    def wanted(shape, dim, d, core):
        at = lax.broadcasted_iota(jnp.int32, shape, dim)
        j = quotient(at, far_rows, shape[dim])
        place = at - j * far_rows
        pos = z + toward[d] * (relay + 1 + j)
        pos = jnp.where(pos < 0, pos + nz, pos)
        pos = jnp.where(pos >= nz, pos - nz, pos)
        place = place - core * cap
        held = (place >= 0) & (place < cap)
        return jnp.where(held, (pos * 2 + c) * cap + place, -5).astype(f32)

    def write_onehots(s):
        ids = lax.broadcasted_iota(jnp.int32, (rows, toks), 0).astype(f32)
        for d in ways:
            base = ((at_z(z + toward[d] * (relay - s)) * 2 + c) * rows).astype(f32)
            for h in (0, 1):
                onehots[rows * d : rows * (d + 1), toks * h : toks * (h + 1)] = (
                    (code[h, 0:1, :] == ids + base).astype(f32).astype(bf16)
                )

    def add_up(i):
        contrib[:, cols[i]] = jnp.dot(
            onehots[...], tok[:, cols[i]], preferred_element_type=f32
        )

    def own_terms(i):
        return contrib[:, cols[i]].reshape(2, rows, PIECE)

    def send_on(i, s, x):
        packed, levels = quantise(x)
        ref = ring_out.at[i, lax.rem(s, 2)]
        ref[:, 0:rows, :] = packed
        ref[:, rows : rows + 1, :] = levels
        for d in ways:
            ring_copy(i, d, s).start()

    def arrived(i, s):
        for d in ways:
            ring_copy(i, d, s).wait_recv()
        ref = ring_in.at[i, s]
        return unpack(ref[:, 0:rows, :], ref[:, rows : rows + 1, :])

    def relay_step(i):
        x = own_terms(i)
        if far_all:
            for k in range(far_all):
                far_copy(i, k).wait_recv()
            ref = far_in.at[i]
            ids = ref[:, both + 1 : both + 2, :]
            spread = unpack(ref[...], ref[:, both : both + 1, :])
            lane = lax.broadcasted_iota(jnp.int32, (1, LANES), 1)
            sub = lax.broadcasted_iota(jnp.int32, (rows, LANES), 0)
            placed = []
            for d in ways:
                ks = slice(far[LONGER] * d, far[LONGER] + far[SHORTER] * d)
                n = far[d] * far_rows
                ids_d = jnp.sum(ids[ks], axis=0) if n else jnp.zeros_like(lane)
                placing = ((jnp.where(lane < n, ids_d, -1)) == sub).astype(f32)
                parts = [spread[ks].reshape(n, PIECE)] if n else []
                if n < LANES:
                    parts.append(jnp.zeros((LANES - n, PIECE), f32))
                y = jnp.concatenate(parts, axis=0)
                top = y.astype(bf16)
                rest = (y - top.astype(f32)).astype(bf16)
                placing = placing.astype(bf16)
                placed.append(
                    jnp.dot(placing, top, preferred_element_type=f32)
                    + jnp.dot(placing, rest, preferred_element_type=f32)
                )
            x = x + jnp.stack(placed)
        send_on(i, 0, x)

    pair_code.wait_recv()
    write_onehots(0)
    at = 0
    for d in ways:
        n = far[d] * far_rows
        if not n:
            continue
        for h in (0, 1):
            slots_of = wanted((n, LANES), 0, d, h)
            far_onehot[at : at + n, toks * h : toks * (h + 1)] = jnp.concatenate(
                [
                    (slots_of == code[h, 1:2, LANES * k : LANES * (k + 1)]).astype(f32)
                    for k in range(toks // LANES)
                ],
                axis=1,
            ).astype(bf16)
        found = jnp.zeros((8, LANES), f32)
        for h in (0, 1):
            sub = lax.broadcasted_iota(jnp.int32, (toks, LANES), 0).astype(f32)
            choose = (wanted((1, LANES), 1, d, h) == sub).astype(f32)
            found = found + jnp.dot(
                jnp.broadcast_to(code[h, 2:3, :], (8, toks)).astype(bf16),
                choose.astype(bf16),
                preferred_element_type=f32,
            )
        lane = lax.broadcasted_iota(jnp.int32, (1, LANES), 1)
        which = quotient(lane, far_rows, LANES)
        ids = jnp.where(
            lane - which * far_rows < both, found[0:1, :].astype(jnp.int32), -1
        )
        for j in range(far[d]):
            far_ids[far[LONGER] * d + j] = jnp.where(which == j, ids, 0)
        at += n

    def tokens_in(i):
        if i == 0:
            own_tok.wait()

        @pl.loop(1, n_node)
        def _(j):
            tok_copy(i, j, True).wait_recv()

        tok[0:toks, cols[i]] = jnp.concatenate(
            [tok3[n, :, cols[i]].astype(f32) for n in range(n_node)], axis=0
        ).astype(bf16)
        pair_copy(i).start()

    def far_rows_out(i):
        pair_copy(i).wait_recv()
        if far_all:
            x = jnp.dot(far_onehot[...], tok[:, cols[i]], preferred_element_type=f32)
            packed, levels = quantise(x.reshape(far_all, far_rows, PIECE))
            at = lax.broadcasted_iota(jnp.int32, packed.shape, 1)
            far_out[i] = jnp.where(
                at == both,
                levels,
                jnp.where(at == both + 1, far_ids[...], packed),
            )
            for k in range(far_all):
                far_copy(i, k).start()
        add_up(i)

    for i in range(pieces):
        tokens_in(i)
        if i:
            far_rows_out(i - 1)
    far_rows_out(pieces - 1)
    for i in range(pieces):
        relay_step(i)
    write_onehots(1)
    for i in range(pieces):
        add_up(i)

    @pl.loop(1, relay)
    def _(s):
        for i in range(pieces):
            for d in ways:
                ring_copy(i, d, s - 1).wait_recv()
                ref = ring_in.at[i, s - 1, d]
                x = unpack(ref[0:rows, :], ref[rows : rows + 1, :])
                x = x + contrib[rows * d : rows * (d + 1), cols[i]]

                @pl.when(s >= 2)
                def _(i=i, d=d):
                    ring_copy(i, d, s - 2).wait_send()

                packed, levels = quantise(x)
                ref = ring_out.at[i, lax.rem(s, 2), d]
                ref[0:rows, :] = packed
                ref[rows : rows + 1, :] = levels
                ring_copy(i, d, s).start()
        write_onehots(s + 1)
        for i in range(pieces):
            add_up(i)

    for i in range(pieces):
        x = arrived(i, relay - 1)
        out[:, cols[i]] = x[0] + x[1] + contrib[0:rows, cols[i]]

    @pl.loop(1, n_node)
    def _(j):
        slot_copy(j, False).wait_send()
        for i in range(pieces):
            tok_copy(i, j, False).wait_send()

    pair_code.wait_send()
    for i in range(pieces):
        pair_copy(i).wait_send()
        for k in range(far_all):
            far_copy(i, k).wait_send()
        for d in ways:
            for s in range(max(relay - 2, 0), relay):
                ring_copy(i, d, s).wait_send()


def summed(grads, merge_slot, slot_row, n_group, n_node, rows):
    toks, width = grads.shape
    blk = toks // n_node
    pieces = width // PIECE
    assert width == PIECE * pieces
    _, relay, far, both, far_rows = plan(n_group, toks)
    far_all = max(far[LONGER] + far[SHORTER], 1)
    assert far[LONGER] * far_rows <= LANES
    cfg = (n_group, n_node, rows, toks, width)
    i32, f32, bf16 = jnp.int32, jnp.float32, jnp.bfloat16
    vmem, dma = pltpu.VMEM, pltpu.SemaphoreType.DMA
    return pl.pallas_call(
        functools.partial(kernel, cfg),
        out_shape=jax.ShapeDtypeStruct((rows, width), f32),
        in_specs=[
            pl.BlockSpec(memory_space=pltpu.HBM),
            pl.BlockSpec(memory_space=vmem),
            pl.BlockSpec(memory_space=vmem),
        ],
        out_specs=pl.BlockSpec(memory_space=vmem),
        scratch_shapes=[
            vmem((n_node, blk, width), bf16),
            vmem((n_node, toks // LANES, LANES), i32),
            vmem((2 * toks, width), bf16),
            vmem((2, 3, toks), f32),
            vmem((n_node, toks), i32),
            vmem((2 * rows, 2 * toks), bf16),
            vmem((2 * rows, width), f32),
            vmem((far_all * far_rows, 2 * toks), bf16),
            vmem((far_all, 1, LANES), i32),
            vmem((pieces, far_all, far_rows, LANES), i32),
            vmem((pieces, far_all, far_rows, LANES), i32),
            vmem((pieces, 2, 2, rows + 1, LANES), i32),
            vmem((pieces, relay, 2, rows + 1, LANES), i32),
            dma((n_node,)),
            dma((n_node,)),
            dma((pieces, n_node)),
            dma((pieces, n_node)),
            dma((2,)),
            dma((pieces + 1,)),
            dma((pieces + 1,)),
            dma((pieces, far_all)),
            dma((pieces, far_all)),
            dma((pieces, 2, 2)),
            dma((pieces, 2, relay)),
        ],
        compiler_params=pltpu.CompilerParams(
            collective_id=0, has_side_effects=True, vmem_limit_bytes=40 * 1024 * 1024
        ),
        name="ring_sums",
    )(
        grads.reshape(n_node, blk, width),
        merge_slot.reshape(toks // LANES, LANES),
        slot_row.reshape(toks // LANES, LANES),
    )


def on_device(n_group, n_node, grads, merge_slot, slot_row, params, moment, second):
    grad = summed(grads, merge_slot, slot_row, n_group, n_node, params.shape[0])
    new_moment = 0.9 * moment + 0.1 * grad
    new_second = 0.999 * second + 0.001 * grad * grad
    first_fix = 1.0 - 0.9**10
    second_fix = 1.0 - 0.999**10
    new_params = params - 0.1 * (new_moment / first_fix) / (
        jnp.sqrt(new_second / second_fix) + 1e-08
    )
    return (new_params, new_moment, new_second)


def solution(mesh):
    whole, flat = P(("group", "node"), None), P(("group", "node"))
    return jax.shard_map(
        functools.partial(on_device, mesh.shape["group"], mesh.shape["node"]),
        mesh=mesh,
        in_specs=(whole, flat, flat, whole, whole, whole),
        out_specs=(whole, whole, whole),
        check_vma=False,
    )
```

time: 113 us -> 94.4 us (0.84)
  the two profiles are of different devices: /device:TPU:32 before, /device:TPU:8 now
where the time goes in v2:
time: 94.4 us; the launch traced here: 94.2 us
  Pallas kernels  90.6 us (96%)
  local copies, waits for them, and re-layouts  1.89 us (2%)
  other arithmetic  1.07 us (1%)
    pallas_call x1, Pallas kernels, summed(): pl.pallas_call(functools.partial(kernel, cfg), out_shape=jax.ShapeDtypeSt...  90.6 us
    unnamed x12, local copies, waits for them, and re-layouts  1.89 us

profile of v2, /device:TPU:8, one launch (start us, length us, event | category | flops | bytes accessed | tf_op | source)
XLA Modules:
  0.0 94.2 jit_solution(2240561605903324846)
XLA Ops:
  0.6 0.0 copy-start.2
  0.6 0.0 copy-start.1
  0.7 0.7 copy-done.2
  1.3 0.0 copy-done.1
  1.3 0.0 copy-start
  1.3 1.2 %copy-done = bf16[384,1280]{1,0:T(8,128)(2,1)S(1)} copy-done((bf16[384,1280]{1,0:T(8,128)(2,1)S(1)}, bf16[384,1280]{1,0:T(8,128)(2,1)}, u32[]{:S(2)}) %copy-start) | copy-done | bytes 983064
  2.5 0.0 copy-start.3
  2.5 0.0 copy-start.4
  2.5 0.0 copy-start.5
  2.5 90.6 %ring_sums.1 = f32[64,1280]{1,0:T(8,128)S(1)} custom-call(bf16[16,24,1280]{2,1,0:T(8,128)(2,1)S(1)} %bitcast.3, s32[3,128]{1,0:T(4,128)S(1)} %bitcast.4, s32[3,128]{1,0:T(4,128)S(1)} %bitcast.5), custom_call_target="tpu_custom_call" | custom-call | tf_op jit(solution)/shard_map/ring_sums/pallas_call | solution.py:464
  93.1 0.0 copy-done.3
  93.1 0.0 copy-done.4
  93.1 0.0 copy-done.5
  93.2 1.1 %divide_subtract_fusion = (f32[64,1280]{1,0:T(8,128)}, f32[64,1280]{1,0:T(8,128)}, f32[64,1280]{1,0:T(8,128)}) fusion(f32[64,1280]{1,0:T(8,128)S(1)} %copy-done.3, f32[64,1280]{1,0:T(8,128)S(1)} %ring_sums.1, f32[64,1280]{1,0:T(8,128)S(1)} %copy-done.4, f32[64,1280]{1,0:T(8,128)S(1)} %copy-done.5), kind=kLoop, calls=%fused_computation.2 | loop fusion | flops 983040 | bytes 2293760 | tf_op jit(solution)/shard_map/sub | solution.py:516
Async XLA Ops:
  0.6 0.7 copy-start.2
  0.6 0.7 copy-start.1
  1.3 1.2 %copy-start = (bf16[384,1280]{1,0:T(8,128)(2,1)S(1)}, bf16[384,1280]{1,0:T(8,128)(2,1)}, u32[]{:S(2)}) copy-start(bf16[384,1280]{1,0:T(8,128)(2,1)} %param.6) | copy-start | bytes 2949124
  2.5 90.6 %copy-start.3 = (f32[64,1280]{1,0:T(8,128)S(1)}, f32[64,1280]{1,0:T(8,128)}, u32[]{:S(2)}) copy-start(f32[64,1280]{1,0:T(8,128)} %param.9) | copy-start | bytes 983044
  2.5 90.6 %copy-start.4 = (f32[64,1280]{1,0:T(8,128)S(1)}, f32[64,1280]{1,0:T(8,128)}, u32[]{:S(2)}) copy-start(f32[64,1280]{1,0:T(8,128)} %param.10) | copy-start | bytes 983044
  2.5 90.6 %copy-start.5 = (f32[64,1280]{1,0:T(8,128)S(1)}, f32[64,1280]{1,0:T(8,128)}, u32[]{:S(2)}) copy-start(f32[64,1280]{1,0:T(8,128)} %param.11) | copy-start | bytes 983044

commit v3 on v2

--- a/solution.py
+++ b/solution.py
@@ -57,7 +57,7 @@
 def plan(n_group, toks):
     nz = n_group // 2
     hops = (nz // 2, nz // 2 - 1)
-    relay = 12 if nz == 32 else max(nz // 2 - 2, 1)
+    relay = 11 if nz == 32 else max(nz // 2 - 2, 1)
     far = (hops[0] - relay, hops[1] - relay)
     both = 2 * (toks // n_group)
     return nz, relay, far, both, -(-(both + 2) // 8) * 8
@@ -393,7 +393,7 @@
                 levels,
                 jnp.where(at == both + 1, far_ids[...], packed),
             )
-            for k in range(far_all):
+            for k in reversed(range(far_all)):
                 far_copy(i, k).start()
         add_up(i)
 

time: 94.4 us -> 93 us (0.985)
  Pallas kernels: 90.6 us -> 89.2 us
    pallas_call x1, Pallas kernels: 90.6 us -> 89.2 us  [summed(): pl.pallas_call(functools.partial(kernel, cfg), out_shape=jax.ShapeDtypeSt...]
where the time goes in v3:
time: 93 us; the launch traced here: 92.8 us
  Pallas kernels  89.2 us (96%)
  local copies, waits for them, and re-layouts  1.89 us (2%)
  other arithmetic  1.07 us (1%)
    pallas_call x1, Pallas kernels, summed(): pl.pallas_call(functools.partial(kernel, cfg), out_shape=jax.ShapeDtypeSt...  89.2 us
    unnamed x12, local copies, waits for them, and re-layouts  1.89 us

profile of v3, /device:TPU:8, one launch (start us, length us, event | category | flops | bytes accessed | tf_op | source)
XLA Modules:
  0.0 92.8 jit_solution(5271419696807770247)
XLA Ops:
  0.6 0.0 copy-start.2
  0.6 0.0 copy-start.1
  0.7 0.7 copy-done.2
  1.3 0.0 copy-done.1
  1.3 0.0 copy-start
  1.3 1.2 %copy-done = bf16[384,1280]{1,0:T(8,128)(2,1)S(1)} copy-done((bf16[384,1280]{1,0:T(8,128)(2,1)S(1)}, bf16[384,1280]{1,0:T(8,128)(2,1)}, u32[]{:S(2)}) %copy-start) | copy-done | bytes 983064
  2.5 0.0 copy-start.3
  2.5 0.0 copy-start.4
  2.5 0.0 copy-start.5
  2.5 89.2 %ring_sums.1 = f32[64,1280]{1,0:T(8,128)S(1)} custom-call(bf16[16,24,1280]{2,1,0:T(8,128)(2,1)S(1)} %bitcast.3, s32[3,128]{1,0:T(4,128)S(1)} %bitcast.4, s32[3,128]{1,0:T(4,128)S(1)} %bitcast.5), custom_call_target="tpu_custom_call" | custom-call | tf_op jit(solution)/shard_map/ring_sums/pallas_call | solution.py:464
  91.7 0.0 copy-done.3
  91.7 0.0 copy-done.4
  91.7 0.0 copy-done.5
  91.7 1.1 %divide_subtract_fusion = (f32[64,1280]{1,0:T(8,128)}, f32[64,1280]{1,0:T(8,128)}, f32[64,1280]{1,0:T(8,128)}) fusion(f32[64,1280]{1,0:T(8,128)S(1)} %copy-done.3, f32[64,1280]{1,0:T(8,128)S(1)} %ring_sums.1, f32[64,1280]{1,0:T(8,128)S(1)} %copy-done.4, f32[64,1280]{1,0:T(8,128)S(1)} %copy-done.5), kind=kLoop, calls=%fused_computation.2 | loop fusion | flops 983040 | bytes 2293760 | tf_op jit(solution)/shard_map/sub | solution.py:516
Async XLA Ops:
  0.6 0.7 copy-start.2
  0.6 0.7 copy-start.1
  1.3 1.2 %copy-start = (bf16[384,1280]{1,0:T(8,128)(2,1)S(1)}, bf16[384,1280]{1,0:T(8,128)(2,1)}, u32[]{:S(2)}) copy-start(bf16[384,1280]{1,0:T(8,128)(2,1)} %param.6) | copy-start | bytes 2949124
  2.5 89.2 %copy-start.3 = (f32[64,1280]{1,0:T(8,128)S(1)}, f32[64,1280]{1,0:T(8,128)}, u32[]{:S(2)}) copy-start(f32[64,1280]{1,0:T(8,128)} %param.9) | copy-start | bytes 983044
  2.5 89.2 %copy-start.4 = (f32[64,1280]{1,0:T(8,128)S(1)}, f32[64,1280]{1,0:T(8,128)}, u32[]{:S(2)}) copy-start(f32[64,1280]{1,0:T(8,128)} %param.10) | copy-start | bytes 983044
  2.5 89.2 %copy-start.5 = (f32[64,1280]{1,0:T(8,128)S(1)}, f32[64,1280]{1,0:T(8,128)}, u32[]{:S(2)}) copy-start(f32[64,1280]{1,0:T(8,128)} %param.11) | copy-start | bytes 983044
